TPU v7x, 256 devices: a whole 4x4x8 slice. The times are simulated.
256 devices in a mesh: dp: 16 (over x, z_hi), tensor: 16 (over z_lo, y, core).
Axes of the slice: x: 4, y: 4, z: 8 (z_hi: 4, z_lo: 2; z = z_hi * 2 + z_lo), core: 2. Of those that a mesh axis runs over, the one named last changes fastest.
Arguments:
- inputs: bfloat16 [32768, 28672], P('dp', 'tensor'), may hold values from -6 to 6
- out_grads: bfloat16 [32768, 8192], P(('dp', 'tensor')), may hold values from -6 to 6
- proj_in: bfloat16 [28672, 64], P('tensor'), may hold values from -0.03125 to 0.03125
- proj_out: bfloat16 [8192, 64], replicated, may hold values from -0.0625 to 0.0625
- example_ids: int32 [16, 2048], P('dp'), may hold values from 0 to 3, never falling along the last dimension, each value on 1 to 768 neighbouring positions
Outputs:
- covariance: float32 [4096, 4096], P('dp', 'tensor')
Inputs may be any that keep to these rules, and one draw needn't show every extreme that they name: `example_ids`: along each group the example number never falls; each of the 4 examples has 1 to 768 tokens and in every group one has exactly 768.
All inputs are finite; a program needn't handle non-finite values.
Results may differ from a plain program's by a relative error of at most 0.0003.
Values sent between devices are 32-bit elements; how exact they have to be, the bound alone decides.
A program may use at most 64 MiB of HBM per device.

v0:
```python
import jax
import jax.numpy as jnp
from jax import lax
from jax.sharding import PartitionSpec as P

SEQ = 512
EX_DEV = 4


def partial_grads(sketch_cols, grad_cols, token_ids):
    labels = jnp.arange(EX_DEV, dtype=jnp.int32)
    onehot = (token_ids[None, :] == labels[:, None]).astype(jnp.float32)
    width = sketch_cols.shape[0]
    weighted = (sketch_cols[None, :, :] * onehot[:, None, :]).reshape(
        EX_DEV * width, sketch_cols.shape[1]
    )
    return lax.dot_general(
        weighted,
        grad_cols,
        (((1,), (1,)), ((), ())),
        precision=lax.Precision.HIGHEST,
        preferred_element_type=jnp.float32,
    )


def per_device(inputs, out_grads, proj_in, proj_out, example_ids):
    width = proj_in.shape[1]
    token_share = out_grads.shape[0]
    tensor_index = lax.axis_index("tensor")
    group_index = lax.axis_index("dp")
    token_ids = example_ids[0]
    own_ids = lax.dynamic_slice_in_dim(token_ids, tensor_index * token_share, token_share, 0)
    grad_sketch = lax.dot_general(
        proj_out, out_grads, (((0,), (1,)), ((), ())), preferred_element_type=jnp.float32
    )
    partial_value = lax.dot_general(
        proj_in, inputs, (((0,), (1,)), ((), ())), preferred_element_type=jnp.float32
    )
    summed = lax.psum(partial_value, "tensor")
    own_cols = lax.dynamic_slice_in_dim(summed, tensor_index * token_share, token_share, 1)
    grad_sums = partial_grads(own_cols, grad_sketch, own_ids)
    vectors = lax.psum(grad_sums.reshape(EX_DEV, width * width), "tensor")
    vec_len = width * width
    row_count = vec_len // lax.axis_size("dp")
    col_count = vec_len // lax.axis_size("tensor")
    everyone = lax.all_gather(vectors, "dp", axis=0, tiled=True)
    row_part = lax.dynamic_slice_in_dim(everyone, group_index * row_count, row_count, 1)
    col_part = lax.dynamic_slice_in_dim(everyone, tensor_index * col_count, col_count, 1)
    product = jnp.dot(
        row_part.T, col_part, precision=lax.Precision.HIGHEST, preferred_element_type=jnp.float32
    )
    return product / (row_part.shape[0] * SEQ)


def solution(mesh):
    placed = (P("dp", "tensor"), P(("dp", "tensor"), None), P("tensor", None), P(), P("dp", None))
    return jax.shard_map(
        per_device, mesh=mesh, in_specs=placed, out_specs=P("dp", "tensor"), check_vma=False
    )
```

profile of v0, /device:TPU:33, one launch (start us, length us, event | category | flops | bytes accessed | tf_op | source)
XLA Modules:
  0.0 316.6 jit_solution(17769230258698748167)
XLA Ops:
  6.5 0.0 copy-start
  6.5 0.0 copy-start.1
  6.5 0.0 all-reduce.3.cloned.1.call-start
  6.5 6.5 %fusion.5 = f32[64,2048]{1,0:T(8,128)} fusion(bf16[1792,64]{0,1:T(8,128)(2,1)} %param.7, bf16[2048,1792]{1,0:T(8,128)(2,1)} %param.5), kind=kOutput, calls=%fused_computation.10 | convolution fusion | flops 469762048 | bytes 8093696 | tf_op jit(solution)/shard_map/dot_general | solution.py:36
  13.0 0.0 all-reduce.3.cloned.1.call-update
  13.0 0.0 all-reduce.5.cloned.1.call-start
  13.1 0.7 fusion.4
  13.7 0.0 copy-done
  13.7 0.0 copy-done.1
  13.8 0.8 fusion.6
  14.6 122.3 %all-reduce.3.cloned.1.call-done = f32[64,2048]{1,0:T(8,128)} async-done(((f32[64,2048]{1,0:T(8,128)}), f32[64,2048]{1,0:T(8,128)}) %all-reduce.3.cloned.1.call-update) | async-done | bytes 524304 | tf_op jit(solution)/shard_map/psum | solution.py:39
  136.9 0.8 constant_dynamic-slice_fusion.1
  137.7 0.3 fusion.7
  137.9 0.7 reshape.29
  138.7 0.0 all-reduce.5.cloned.1.call-update
  138.7 0.0 all-gather.3.cloned.1.call-start
  138.8 112.5 %all-reduce.5.cloned.1.call-done = f32[4,4096]{1,0:T(4,128)} async-done(((f32[4,4096]{1,0:T(4,128)}), f32[4,4096]{1,0:T(4,128)}) %all-reduce.5.cloned.1.call-update) | async-done | bytes 65552 | tf_op jit(solution)/shard_map/psum | solution.py:42
  251.2 0.0 all-gather.3.cloned.1.call-update
  251.3 56.1 %all-gather.3.cloned.1.call-done = f32[16,4,4096]{2,1,0:T(4,128)} async-done(((f32[1,4,4096]{2,1,0:T(4,128)}), f32[16,4,4096]{2,1,0:T(4,128)}) %all-gather.3.cloned.1.call-update) | async-done | bytes 1048592 | tf_op jit(solution)/shard_map/all_gather | solution.py:46
  307.4 1.6 reshape.31
  309.0 1.1 convolution_multiply_fusion
  (2 shorter events, 0.0 us)
Async XLA Ops:
  6.5 7.2 %copy-start = (bf16[128,8192]{1,0:T(8,128)(2,1)S(1)}, bf16[128,8192]{1,0:T(8,128)(2,1)}, u32[]{:S(2)}) copy-start(bf16[128,8192]{1,0:T(8,128)(2,1)} %param.6) | copy-start | bytes 6291460
  6.5 7.2 %copy-start.1 = (bf16[8192,64]{0,1:T(8,128)(2,1)S(1)}, bf16[8192,64]{0,1:T(8,128)(2,1)}, u32[]{:S(2)}) copy-start(bf16[8192,64]{0,1:T(8,128)(2,1)} %param.8) | copy-start | bytes 3145732
  6.5 130.4 %all-reduce.3.cloned.1.call-start = ((), (), s32[]{:S(2)}) async-start(), calls=%async_computation | async-start | bytes 1048576 | tf_op jit(solution)/shard_map/psum | solution.py:39
  13.0 238.2 %all-reduce.5.cloned.1.call-start = ((), (), s32[]{:S(2)}) async-start(), calls=%async_computation.1 | async-start | bytes 131072 | tf_op jit(solution)/shard_map/psum | solution.py:42
  138.7 168.7 %all-gather.3.cloned.1.call-start = ((), (), s32[]{:S(2)}) async-start(), calls=%async_computation.2 | async-start | bytes 1114112 | tf_op jit(solution)/shard_map/all_gather | solution.py:46
Sparse Core Ops, SparseCore 0:
  13.1 123.7 all-reduce.2
  139.7 111.4 all-reduce.4
  253.7 53.6 all-gather.2
where the time goes:
time: 320 us; the launch traced here: 317 us
  waiting for transfers between devices  291 us (91%)
  between operations  13.1 us (4%)
  matrix products  8.68 us (3%)
  local copies, waits for them, and re-layouts  3.75 us (1%)
    psum x1, waiting for transfers between devices, per_device(): summed = lax.psum(partial_value, 'tensor')  122 us
    psum x1, waiting for transfers between devices, per_device(): vectors = lax.psum(grad_sums.reshape(EX_DEV, width * width), 'tensor')  112 us
    all_gather x1, waiting for transfers between devices, per_device(): everyone = lax.all_gather(vectors, 'dp', axis=0, tiled=True)  56.1 us
    dot_general x1, matrix products, per_device(): lax.dot_general(proj_in, inputs, (((0,), (1,)), ((), ())), preferred_elem...  6.46 us
  transfers between devices with their start and end apart: 3, of which 3 were waited for; matrix products, arithmetic and copies ran while one was open for 0% of the time, Pallas kernels for 0%

commit v1 on v0

v1 whole, which is shorter than its diff:
```python
import jax
import jax.numpy as jnp
from jax import lax
from jax.experimental import pallas as pl
from jax.experimental.pallas import tpu as pltpu
from jax.sharding import PartitionSpec as P

SEQ = 512
EX_DEV = 4
MESH = pl.DeviceIdType.MESH
F32 = jnp.float32
BF16 = jnp.bfloat16
NT = (((1,), (1,)), ((), ()))


def split(x):
    high = x.astype(BF16)
    return high, (x - high.astype(F32)).astype(BF16)


def kernel(
    x_hbm, og_hbm, wi_hbm, wo_hbm, ids_hbm, out_ref,
    x_v, og_v, wi_v, wo_v, ids_v, g_v, give, take, masked, pieces, shares, mine, cols, rows,
    local_sem, x_sem, g_send, g_recv, s_send, s_recv, b_send, b_recv, c_send, col_recv, row_recv,
):
    dp = lax.axis_index("dp")
    tensor = lax.axis_index("tensor")
    core = lax.rem(tensor, 2)
    chip = lax.div(tensor, 2)
    partner = (dp, tensor + 1 - 2 * core)

    og_copy = pltpu.make_async_copy(og_hbm, og_v, local_sem.at[0])
    wo_copy = pltpu.make_async_copy(wo_hbm, wo_v, local_sem.at[1])
    wi_copy = pltpu.make_async_copy(wi_hbm, wi_v, local_sem.at[2])
    ids_copy = pltpu.make_async_copy(ids_hbm, ids_v, local_sem.at[3])
    wo_copy.start()
    og_copy.start()
    wi_copy.start()
    ids_copy.start()
    x_copies = []
    for half in range(2):
        parity = (1 - core) if half == 0 else core
        for b in range(8):
            slot = half * 8 + b
            copy = pltpu.make_async_copy(
                x_hbm.at[pl.ds(pl.multiple_of((2 * b + parity) * 128, 128), 128), :],
                x_v.at[slot],
                x_sem.at[slot],
            )
            copy.start()
            x_copies.append(copy)

    barrier = pltpu.get_barrier_semaphore()

    def greet(rel, carry):
        pl.semaphore_signal(barrier, inc=1, device_id=(dp, lax.rem(tensor + rel, 16)), device_id_type=MESH)
        pl.semaphore_signal(barrier, inc=1, device_id=(lax.rem(dp + rel, 16), tensor), device_id_type=MESH)
        pl.semaphore_signal(barrier, inc=1, device_id=(lax.rem(dp + rel, 16), dp), device_id_type=MESH)
        return carry

    lax.fori_loop(1, 16, greet, 0)

    @pl.when(tensor != dp)
    def _():
        pl.semaphore_signal(barrier, inc=1, device_id=(dp, dp), device_id_type=MESH)

    wo_copy.wait()
    og_copy.wait()
    g_v[chip] = lax.dot_general(wo_v[...], og_v[...], NT, preferred_element_type=F32)

    pl.semaphore_wait(barrier, jnp.where(tensor == dp, 45, 46))

    g_copies = []
    for rel in range(1, 8):
        peer = lax.rem(chip + rel, 8)
        copy = pltpu.make_async_remote_copy(
            src_ref=g_v.at[chip], dst_ref=g_v.at[chip], send_sem=g_send.at[rel], recv_sem=g_recv.at[rel],
            device_id=(dp, 2 * peer + core), device_id_type=MESH,
        )
        copy.start()
        g_copies.append(copy)

    wi_copy.wait()
    ids_copy.wait()
    s_copies = []
    for pair in range(4):
        x_copies[2 * pair].wait()
        x_copies[2 * pair + 1].wait()
        block = x_v[2 * pair : 2 * pair + 2].reshape(256, 1792)
        sketch = lax.dot_general(wi_v[...], block, NT, preferred_element_type=F32)
        give[2 * pair] = sketch[:, :128]
        give[2 * pair + 1] = sketch[:, 128:]
        copy = pltpu.make_async_remote_copy(
            src_ref=give.at[pl.ds(2 * pair, 2)], dst_ref=take.at[pl.ds(2 * pair, 2)],
            send_sem=s_send.at[pair], recv_sem=s_recv.at[pair], device_id=partner, device_id_type=MESH,
        )
        copy.start()
        s_copies.append(copy)
    for pair in range(4):
        x_copies[8 + 2 * pair].wait()
        x_copies[8 + 2 * pair + 1].wait()
        block = x_v[8 + 2 * pair : 8 + 2 * pair + 2].reshape(256, 1792)
        sketch = lax.dot_general(wi_v[...], block, NT, preferred_element_type=F32)
        s_copies[pair].wait_recv()
        for k in range(2):
            b = 2 * pair + k
            total = sketch[:, 128 * k : 128 * (k + 1)] + take[b]
            ids = ids_v[:, pl.ds(pl.multiple_of((2 * b + core) * 128, 128), 128)]
            high, low = split(total)
            for e in range(EX_DEV):
                own = ids == e
                lanes = slice(128 * b, 128 * (b + 1))
                masked[64 * e : 64 * (e + 1), lanes] = jnp.where(own, high, jnp.zeros_like(high))
                masked[256 + 64 * e : 256 + 64 * (e + 1), lanes] = jnp.where(own, low, jnp.zeros_like(low))

    for copy in g_copies:
        copy.wait_recv()
    grads = []
    for b in range(8):
        high, low = split(g_v[b])
        grads.append(jnp.concatenate([high, low], axis=0))
    product = lax.dot_general(
        masked[...], jnp.concatenate(grads, axis=1), NT, preferred_element_type=F32
    )
    lane = lax.broadcasted_iota(jnp.int32, (64, 128), 1)
    both = []
    for e in range(EX_DEV):
        term = product[64 * e : 64 * (e + 1)] + product[256 + 64 * e : 256 + 64 * (e + 1)]
        both.append(term + pltpu.roll(term, 64, 1))
    first = jnp.where(lane < 64, both[0], both[1]).reshape(8, 8, 128)
    second = jnp.where(lane < 64, both[2], both[3]).reshape(8, 8, 128)
    row8 = lax.broadcasted_iota(jnp.int32, (8, 8, 128), 1)
    even = jnp.where(row8 < 4, first, pltpu.roll(second, 4, 1))
    odd = jnp.where(row8 < 4, pltpu.roll(first, 4, 1), second)
    for u in range(8):
        pieces[2 * u] = even[u]
        pieces[2 * u + 1] = odd[u]

    shares[tensor] = pieces[tensor]
    b_copies = []
    for rel in range(1, 16):
        peer = lax.rem(tensor + rel, 16)
        copy = pltpu.make_async_remote_copy(
            src_ref=pieces.at[peer], dst_ref=shares.at[tensor], send_sem=b_send.at[rel], recv_sem=b_recv.at[rel],
            device_id=(dp, peer), device_id_type=MESH,
        )
        copy.start()
        b_copies.append(copy)
    for copy in b_copies:
        copy.wait_recv()
    total = shares[0]
    for k in range(1, 16):
        total = total + shares[k]
    row = lax.broadcasted_iota(jnp.int32, (8, 128), 0) % 2
    side = lax.broadcasted_iota(jnp.int32, (8, 128), 1) // 64
    swapped = pltpu.roll(total, 64, 1)
    piece = jnp.where(
        row == side, total, jnp.where(row == 0, pltpu.roll(swapped, 7, 0), pltpu.roll(swapped, 1, 0))
    )
    mine[...] = piece

    cols[dp] = piece

    c_copies = []
    for rel in range(1, 16):
        copy = pltpu.make_async_remote_copy(
            src_ref=mine, dst_ref=cols.at[dp], send_sem=c_send.at[rel], recv_sem=col_recv.at[rel],
            device_id=(lax.rem(dp + rel, 16), tensor), device_id_type=MESH,
        )
        copy.start()
        c_copies.append(copy)
    row_copies = []
    for rel in range(1, 16):
        copy = pltpu.make_async_remote_copy(
            src_ref=mine, dst_ref=rows.at[dp], send_sem=c_send.at[16 + rel], recv_sem=row_recv.at[dp],
            device_id=(tensor, lax.rem(dp + rel, 16)), device_id_type=MESH,
        )
        copy.start()
        row_copies.append(copy)
    last = pltpu.make_async_remote_copy(
        src_ref=mine, dst_ref=rows.at[dp], send_sem=c_send.at[16], recv_sem=row_recv.at[dp],
        device_id=(tensor, dp), device_id_type=MESH,
    )

    @pl.when(tensor != dp)
    def _():
        last.start()

    @pl.when(tensor == dp)
    def _():
        rows[dp] = piece

    for copy in c_copies:
        copy.wait_recv()
    for g in range(16):
        @pl.when(jnp.logical_or(tensor != dp, dp != g))
        def _():
            pltpu.make_async_copy(rows.at[g], rows.at[g], row_recv.at[g]).wait()

    r2 = rows[...].reshape(128, 128).T
    c2 = cols[...].reshape(128, 128)
    r_bit = (lax.broadcasted_iota(jnp.int32, (128, 128), 1) // 2) % 2
    c_bit = (lax.broadcasted_iota(jnp.int32, (128, 128), 0) // 2) % 2
    zero = jnp.zeros_like(r2)
    left = jnp.concatenate([jnp.where(r_bit == 0, r2, zero), jnp.where(r_bit == 1, r2, zero)], axis=0)
    right = jnp.concatenate(
        [jnp.where(c_bit == 0, c2, pltpu.roll(c2, 2, 0)), jnp.where(c_bit == 1, c2, pltpu.roll(c2, 126, 0))], axis=1
    )
    lh, ll = split(left)
    rh, rl = split(right)
    dot = lambda a, b: jnp.dot(a, b, preferred_element_type=F32)
    out_ref[...] = (dot(lh, rl) + dot(ll, rh) + dot(lh, rh)) * (1.0 / (64 * SEQ))

    for copy in g_copies + s_copies + b_copies + c_copies + row_copies:
        copy.wait_send()

    @pl.when(tensor != dp)
    def _():
        last.wait_send()


def per_device(inputs, out_grads, proj_in, proj_out, example_ids):
    any_space = pl.BlockSpec(memory_space=pl.ANY)
    dma = pltpu.SemaphoreType.DMA
    return pl.pallas_call(
        kernel,
        out_shape=jax.ShapeDtypeStruct((256, 256), F32),
        in_specs=[any_space] * 5,
        out_specs=pl.BlockSpec(memory_space=pltpu.VMEM),
        scratch_shapes=[
            pltpu.VMEM((16, 128, 1792), BF16),
            pltpu.VMEM((128, 8192), BF16),
            pltpu.VMEM((64, 1792), BF16),
            pltpu.VMEM((64, 8192), BF16),
            pltpu.VMEM((1, 2048), jnp.int32),
            pltpu.VMEM((8, 64, 128), F32),
            pltpu.VMEM((8, 64, 128), F32),
            pltpu.VMEM((8, 64, 128), F32),
            pltpu.VMEM((512, 1024), BF16),
            pltpu.VMEM((16, 8, 128), F32),
            pltpu.VMEM((16, 8, 128), F32),
            pltpu.VMEM((8, 128), F32),
            pltpu.VMEM((16, 8, 128), F32),
            pltpu.VMEM((16, 8, 128), F32),
            dma((4,)), dma((16,)), dma((8,)), dma((8,)), dma((4,)), dma((4,)),
            dma((16,)), dma((16,)), dma((32,)), dma((16,)), dma((16,)),
        ],
        compiler_params=pltpu.CompilerParams(
            collective_id=0, has_side_effects=True, vmem_limit_bytes=48 * 1024 * 1024
        ),
        cost_estimate=pl.CostEstimate(flops=10**9, bytes_accessed=12 * 10**6, transcendentals=0),
    )(inputs, out_grads, proj_in.T, proj_out.T, example_ids)


def solution(mesh):
    placed = (P("dp", "tensor"), P(("dp", "tensor"), None), P("tensor", None), P(), P("dp", None))
    return jax.shard_map(
        per_device, mesh=mesh, in_specs=placed, out_specs=P("dp", "tensor"), check_vma=False
    )
```

time: 320 us -> 36.8 us (0.11)
  the two profiles are of different devices: /device:TPU:33 before, /device:TPU:7 now
where the time goes in v1:
time: 36.8 us; the launch traced here: 36.6 us
  Pallas kernels  31.4 us (85%)
  local copies, waits for them, and re-layouts  5.15 us (14%)
    pallas_call x1, Pallas kernels, per_device(): pl.pallas_call(kernel, out_shape=jax.ShapeDtypeStruct((256, 256), F32), i...  31.4 us
    unnamed x9, local copies, waits for them, and re-layouts  5.15 us

profile of v1, /device:TPU:7, one launch (start us, length us, event | category | flops | bytes accessed | tf_op | source)
XLA Modules:
  0.0 36.6 jit_solution(11205029585703735162)
XLA Ops:
  0.0 0.0 copy-start
  0.0 1.6 %copy-done = bf16[128,8192]{1,0:T(8,128)(2,1)S(1)} copy-done((bf16[128,8192]{1,0:T(8,128)(2,1)S(1)}, bf16[128,8192]{1,0:T(8,128)(2,1)}, u32[]{:S(2)}) %copy-start) | copy-done | bytes 2097176
  1.6 0.0 copy-start.1
  1.6 1.2 %copy-done.1 = bf16[8192,64]{0,1:T(8,128)(2,1)S(1)} copy-done((bf16[8192,64]{0,1:T(8,128)(2,1)S(1)}, bf16[8192,64]{0,1:T(8,128)(2,1)}, u32[]{:S(2)}) %copy-start.1) | copy-done | bytes 1048600
  2.8 0.0 copy-start.2
  2.8 0.9 %copy-done.2 = bf16[1792,64]{0,1:T(8,128)(2,1)S(1)} copy-done((bf16[1792,64]{0,1:T(8,128)(2,1)S(1)}, bf16[1792,64]{0,1:T(8,128)(2,1)}, u32[]{:S(2)}) %copy-start.2) | copy-done | bytes 229400
  3.8 0.0 copy-start.3
  3.8 0.7 %copy-done.3 = s32[1,2048]{1,0:T(1,128)S(1)} copy-done((s32[1,2048]{1,0:T(1,128)S(1)}, s32[1,2048]{1,0:T(1,128)}, u32[]{:S(2)}) %copy-start.3) | copy-done | bytes 8216
  4.5 31.4 %shard_map.55 = f32[256,256]{1,0:T(8,128)S(1)} custom-call(bf16[2048,1792]{1,0:T(8,128)(2,1)} %x_hbm.1, bf16[128,8192]{1,0:T(8,128)(2,1)S(1)} %copy-done, bf16[64,1792]{1,0:T(8,128)(2,1)S(1)} %bitcast.3, bf16[64,8192]{1,0:T(8,128)(2,1)S(1)} %bitcast.2, s32[1,2048]{1,0:T(1,128)S(1)} %copy-done.3), custom_call_target="tpu_custom_call" | custom-call | flops 1000000000 | bytes 12000000 | tf_op jit(solution)/shard_map/pallas_call | solution.py:225
  35.9 0.7 %copy.7 = f32[256,256]{1,0:T(8,128)} copy(f32[256,256]{1,0:T(8,128)S(1)} %shard_map.55) | data formatting | bytes 524288
Async XLA Ops:
  0.0 1.6 %copy-start = (bf16[128,8192]{1,0:T(8,128)(2,1)S(1)}, bf16[128,8192]{1,0:T(8,128)(2,1)}, u32[]{:S(2)}) copy-start(bf16[128,8192]{1,0:T(8,128)(2,1)} %og_hbm.1) | copy-start | bytes 6291460
  1.6 1.2 %copy-start.1 = (bf16[8192,64]{0,1:T(8,128)(2,1)S(1)}, bf16[8192,64]{0,1:T(8,128)(2,1)}, u32[]{:S(2)}) copy-start(bf16[8192,64]{0,1:T(8,128)(2,1)} %param.8) | copy-start | bytes 3145732
  2.8 0.9 %copy-start.2 = (bf16[1792,64]{0,1:T(8,128)(2,1)S(1)}, bf16[1792,64]{0,1:T(8,128)(2,1)}, u32[]{:S(2)}) copy-start(bf16[1792,64]{0,1:T(8,128)(2,1)} %param.7) | copy-start | bytes 688132
  3.8 0.7 %copy-start.3 = (s32[1,2048]{1,0:T(1,128)S(1)}, s32[1,2048]{1,0:T(1,128)}, u32[]{:S(2)}) copy-start(s32[1,2048]{1,0:T(1,128)} %ids_hbm.1) | copy-start | bytes 24580

commit v2 on v1

v2 whole, which is shorter than its diff:
```python
import jax
import jax.numpy as jnp
from jax import lax
from jax.experimental import pallas as pl
from jax.experimental.pallas import tpu as pltpu
from jax.sharding import PartitionSpec as P

SEQ = 512
EX_DEV = 4
MESH = pl.DeviceIdType.MESH
F32 = jnp.float32
BF16 = jnp.bfloat16
NT = (((1,), (1,)), ((), ()))

CHIPS = (6, 5, 7, 2, 4, 1, 3)
TENSORS = (12, 13, 10, 11, 14, 15, 4, 5, 8, 9, 2, 3, 6, 7, 1)
GROUPS = (10, 6, 14, 2, 9, 11, 5, 7, 13, 15, 1, 3, 8, 4, 12)


def split(x):
    high = x.astype(BF16)
    return high, (x - high.astype(F32)).astype(BF16)


def kernel(
    x_hbm, og_hbm, wi_hbm, wo_hbm, ids_hbm, out_ref,
    x_v, og_v, wi_v, wo_v, ids_v, g_v, give, take, masked, pieces, shares, mine, cols, rows,
    local_sem, x_sem, g_send, g_recv, s_send, s_recv, b_send, b_recv, c_send, last_send, col_recv, row_recv,
    x_known, z_known, all_known,
):
    dp = lax.axis_index("dp")
    tensor = lax.axis_index("tensor")
    core = lax.rem(tensor, 2)
    chip = lax.div(tensor, 2)
    y = lax.rem(chip, 4)
    z = lax.div(chip, 4)
    partner = (dp, lax.bitwise_xor(tensor, 1))

    g_reads = []
    for k in range(2):
        half = pl.ds(4096 * k, 4096)
        pair = (
            pltpu.make_async_copy(wo_hbm.at[:, half], wo_v.at[:, half], local_sem.at[2 * k]),
            pltpu.make_async_copy(og_hbm.at[:, half], og_v.at[:, half], local_sem.at[2 * k + 1]),
        )
        for copy in pair:
            copy.start()
        g_reads.append(pair)
    wi_copy = pltpu.make_async_copy(wi_hbm, wi_v, local_sem.at[4])
    ids_copy = pltpu.make_async_copy(ids_hbm, ids_v, local_sem.at[5])
    x_copies = []
    for part in range(4):
        side = lax.bitwise_xor(z, part % 2)
        owner = 1 - core if part < 2 else core
        x_copies.append(pltpu.make_async_copy(x_hbm.at[side, :, owner], x_v.at[part], x_sem.at[part]))

    barrier = pltpu.get_barrier_semaphore()
    x_peers = [(lax.bitwise_xor(dp, 4 * r), tensor) for r in (2, 1, 3)]
    z_peers = [(lax.bitwise_xor(dp, r), tensor) for r in (1, 3)]
    near = [(dp, lax.bitwise_xor(tensor, r)) for r in TENSORS] + x_peers + z_peers
    for peer in near:
        pl.semaphore_signal(barrier, inc=1, device_id=peer, device_id_type=MESH)

    sketch = []
    for k in range(2):
        for copy in g_reads[k]:
            copy.wait()
        if k == 1:
            wi_copy.start()
            ids_copy.start()
            x_copies[0].start()
            x_copies[1].start()
        half = slice(4096 * k, 4096 * (k + 1))
        sketch.append(lax.dot_general(og_v[:, half], wo_v[:, half], NT, preferred_element_type=F32))
    g_v[y] = (sketch[0] + sketch[1]).T

    pl.semaphore_wait(barrier, len(near))
    g_copies = []
    for r in CHIPS:
        copy = pltpu.make_async_remote_copy(
            src_ref=g_v.at[y], dst_ref=g_v.at[4 * (r // 4) + y],
            send_sem=g_send, recv_sem=g_recv.at[r // 4],
            device_id=(dp, 2 * lax.bitwise_xor(chip, r) + core), device_id_type=MESH,
        )
        copy.start()
        g_copies.append(copy)
    for peer in x_peers:
        pl.semaphore_signal(x_known, inc=1, device_id=peer, device_id_type=MESH)

    wi_copy.wait()
    ids_copy.wait()
    s_copies = []
    for part in range(4):
        x_copies[part].wait()
        if part < 2:
            x_copies[part + 2].start()
        sketch = lax.dot_general(
            wi_v[...], x_v[part].reshape(512, 1792), NT, preferred_element_type=F32
        )
        if part < 2:
            give[part] = sketch
            copy = pltpu.make_async_remote_copy(
                src_ref=give.at[part], dst_ref=take.at[part],
                send_sem=s_send.at[part], recv_sem=s_recv.at[part], device_id=partner, device_id_type=MESH,
            )
            copy.start()
            s_copies.append(copy)
            continue
        s_copies[part - 2].wait_recv()
        total = sketch + take[part - 2]
        side = lax.bitwise_xor(z, part % 2)
        ids = jnp.concatenate(
            [ids_v[:, pl.ds(pl.multiple_of((8 * side + 2 * b + core) * 128, 128), 128)] for b in range(4)], axis=1
        )
        high, low = split(total)
        lanes = slice(512 * (part - 2), 512 * (part - 1))
        for e in range(EX_DEV):
            own = ids == e
            masked[64 * e : 64 * (e + 1), lanes] = jnp.where(own, high, jnp.zeros_like(high))
            masked[256 + 64 * e : 256 + 64 * (e + 1), lanes] = jnp.where(own, low, jnp.zeros_like(low))

    pl.semaphore_wait(x_known, len(x_peers))
    for peer in z_peers:
        pl.semaphore_signal(z_known, inc=1, device_id=peer, device_id_type=MESH)

    product = None
    for side in range(2):
        count = 3 if side == 0 else 4
        arrived = g_v.at[pl.ds(0, count)]
        pltpu.make_async_copy(arrived, arrived, g_recv.at[side]).wait()
        grads = []
        for b in range(4):
            high, low = split(g_v[4 * side + b])
            grads.append(jnp.concatenate([high, low], axis=0))
        term = lax.dot_general(
            masked[:, 512 * side : 512 * (side + 1)], jnp.concatenate(grads, axis=1), NT, preferred_element_type=F32
        )
        product = term if side == 0 else product + term
    lane = lax.broadcasted_iota(jnp.int32, (64, 128), 1)
    both = []
    for e in range(EX_DEV):
        term = product[64 * e : 64 * (e + 1)] + product[256 + 64 * e : 256 + 64 * (e + 1)]
        both.append(term + pltpu.roll(term, 64, 1))
    first = jnp.where(lane < 64, both[0], both[1]).reshape(8, 8, 128)
    second = jnp.where(lane < 64, both[2], both[3]).reshape(8, 8, 128)
    row8 = lax.broadcasted_iota(jnp.int32, (8, 8, 128), 1)
    even = jnp.where(row8 < 4, first, pltpu.roll(second, 4, 1))
    odd = jnp.where(row8 < 4, pltpu.roll(first, 4, 1), second)
    for u in range(8):
        pieces[2 * u] = even[u]
        pieces[2 * u + 1] = odd[u]

    for r in TENSORS:
        peer = lax.bitwise_xor(tensor, r)
        pltpu.make_async_remote_copy(
            src_ref=pieces.at[peer], dst_ref=shares.at[r], send_sem=b_send, recv_sem=b_recv,
            device_id=(dp, peer), device_id_type=MESH,
        ).start()
    pl.semaphore_wait(z_known, len(z_peers))
    for peer in z_peers:
        pl.semaphore_signal(all_known, inc=1, device_id=peer, device_id_type=MESH)
    shares[0] = pieces[tensor]
    pl.semaphore_wait(all_known, len(z_peers))
    others = shares.at[pl.ds(1, 15)]
    pltpu.make_async_copy(others, others, b_recv).wait()
    total = shares[0]
    for k in range(1, 16):
        total = total + shares[k]
    row = lax.broadcasted_iota(jnp.int32, (8, 128), 0) % 2
    lane_half = lax.broadcasted_iota(jnp.int32, (8, 128), 1) // 64
    swapped = pltpu.roll(total, 64, 1)
    piece = jnp.where(
        row == lane_half, total, jnp.where(row == 0, pltpu.roll(swapped, 7, 0), pltpu.roll(swapped, 1, 0))
    )
    mine[...] = piece

    for r in TENSORS:
        pltpu.make_async_remote_copy(
            src_ref=mine, dst_ref=rows.at[dp], send_sem=c_send, recv_sem=row_recv,
            device_id=(tensor, lax.bitwise_xor(tensor, r)), device_id_type=MESH,
        ).start()
    for r in GROUPS:
        pltpu.make_async_remote_copy(
            src_ref=mine, dst_ref=cols.at[dp], send_sem=c_send, recv_sem=col_recv,
            device_id=(lax.bitwise_xor(dp, r), tensor), device_id_type=MESH,
        ).start()
    last = pltpu.make_async_remote_copy(
        src_ref=mine, dst_ref=rows.at[dp], send_sem=last_send, recv_sem=row_recv,
        device_id=(tensor, tensor), device_id_type=MESH,
    )
    here = pltpu.make_async_copy(mine, rows.at[dp], row_recv)

    @pl.when(tensor != dp)
    def _():
        last.start()

    @pl.when(tensor == dp)
    def _():
        here.start()

    cols[dp] = piece
    others = cols.at[pl.ds(0, 15)]
    pltpu.make_async_copy(others, others, col_recv).wait()
    pltpu.make_async_copy(rows, rows, row_recv).wait()

    r2 = rows[...].reshape(128, 128).T
    c2 = cols[...].reshape(128, 128)
    r_bit = (lax.broadcasted_iota(jnp.int32, (128, 128), 1) // 2) % 2
    c_bit = (lax.broadcasted_iota(jnp.int32, (128, 128), 0) // 2) % 2
    zero = jnp.zeros_like(r2)
    left = jnp.concatenate([jnp.where(r_bit == 0, r2, zero), jnp.where(r_bit == 1, r2, zero)], axis=0)
    right = jnp.concatenate(
        [jnp.where(c_bit == 0, c2, pltpu.roll(c2, 2, 0)), jnp.where(c_bit == 1, c2, pltpu.roll(c2, 126, 0))], axis=1
    )
    lh, ll = split(left)
    rh, rl = split(right)
    dot = lambda a, b: jnp.dot(a, b, preferred_element_type=F32)
    out_ref[...] = (dot(lh, rl) + dot(ll, rh) + dot(lh, rh)) * (1.0 / (64 * SEQ))

    for copy in s_copies:
        copy.wait_send()
    sent = g_v.at[pl.ds(0, 7)]
    pltpu.make_async_copy(sent, sent, g_send).wait()
    sent = shares.at[pl.ds(0, 15)]
    pltpu.make_async_copy(sent, sent, b_send).wait()
    sent = cols.at[pl.ds(0, 15)]
    pltpu.make_async_copy(sent, sent, c_send).wait()
    pltpu.make_async_copy(sent, sent, c_send).wait()

    @pl.when(tensor != dp)
    def _():
        last.wait_send()


def per_device(inputs, out_grads, proj_in, proj_out, example_ids):
    hbm = pl.BlockSpec(memory_space=pltpu.HBM)
    dma = pltpu.SemaphoreType.DMA
    regular = pltpu.SemaphoreType.REGULAR
    return pl.pallas_call(
        kernel,
        out_shape=jax.ShapeDtypeStruct((256, 256), F32),
        in_specs=[hbm] * 5,
        out_specs=pl.BlockSpec(memory_space=pltpu.VMEM),
        scratch_shapes=[
            pltpu.VMEM((4, 4, 128, 1792), BF16),
            pltpu.VMEM((128, 8192), BF16),
            pltpu.VMEM((64, 1792), BF16),
            pltpu.VMEM((64, 8192), BF16),
            pltpu.VMEM((1, 2048), jnp.int32),
            pltpu.VMEM((8, 64, 128), F32),
            pltpu.VMEM((2, 64, 512), F32),
            pltpu.VMEM((2, 64, 512), F32),
            pltpu.VMEM((512, 1024), BF16),
            pltpu.VMEM((16, 8, 128), F32),
            pltpu.VMEM((16, 8, 128), F32),
            pltpu.VMEM((8, 128), F32),
            pltpu.VMEM((16, 8, 128), F32),
            pltpu.VMEM((16, 8, 128), F32),
            dma((6,)), dma((4,)), dma, dma((2,)), dma((2,)), dma((2,)),
            dma, dma, dma, dma, dma, dma,
            regular, regular, regular,
        ],
        compiler_params=pltpu.CompilerParams(
            collective_id=0, has_side_effects=True, vmem_limit_bytes=57 * 1024 * 1024
        ),
        cost_estimate=pl.CostEstimate(flops=10**9, bytes_accessed=12 * 10**6, transcendentals=0),
    )(inputs.reshape(2, 4, 2, 128, 1792), out_grads, proj_in.T, proj_out.T, example_ids)


def solution(mesh):
    placed = (P("dp", "tensor"), P(("dp", "tensor"), None), P("tensor", None), P(), P("dp", None))
    return jax.shard_map(
        per_device, mesh=mesh, in_specs=placed, out_specs=P("dp", "tensor"), check_vma=False
    )
```

time: 36.8 us -> 30.5 us (0.83)
  the two profiles are of different devices: /device:TPU:7 before, /device:TPU:33 now
where the time goes in v2:
time: 30.5 us; the launch traced here: 30.3 us
  Pallas kernels  28.7 us (94%)
  local copies, waits for them, and re-layouts  1.67 us (5%)
    pallas_call x1, Pallas kernels, per_device(): pl.pallas_call(kernel, out_shape=jax.ShapeDtypeStruct((256, 256), F32), i...  28.7 us
    unnamed x1, local copies, waits for them, and re-layouts  1.67 us

profile of v2, /device:TPU:33, one launch (start us, length us, event | category | flops | bytes accessed | tf_op | source)
XLA Modules:
  0.0 30.3 jit_solution(5263970375553822288)
XLA Ops:
  0.0 28.7 %shard_map.55 = f32[256,256]{1,0:T(8,128)} custom-call(bf16[2,4,2,128,1792]{4,3,2,1,0:T(8,128)(2,1)} %bitcast.3, bf16[128,8192]{1,0:T(8,128)(2,1)} %og_hbm.1, bf16[64,1792]{1,0:T(8,128)(2,1)} %bitcast.5, bf16[64,8192]{1,0:T(8,128)(2,1)} %bitcast.4, s32[1,2048]{1,0:T(1,128)} %ids_hbm.1), custom_call_target="tpu_custom_call" | custom-call | flops 1000000000 | bytes 12000000 | tf_op jit(solution)/shard_map/pallas_call | solution.py:239
  28.7 1.7 %copy.7 = f32[256,256]{1,0:T(8,128)} copy(f32[256,256]{1,0:T(8,128)} %shard_map.55) | data formatting | bytes 524288

commit v3 on v2

--- a/solution.py
+++ b/solution.py
@@ -238,7 +238,7 @@
     regular = pltpu.SemaphoreType.REGULAR
     return pl.pallas_call(
         kernel,
-        out_shape=jax.ShapeDtypeStruct((256, 256), F32),
+        out_shape=pltpu.VMEM((256, 256), F32),
         in_specs=[hbm] * 5,
         out_specs=pl.BlockSpec(memory_space=pltpu.VMEM),
         scratch_shapes=[
@@ -261,10 +261,15 @@
             regular, regular, regular,
         ],
         compiler_params=pltpu.CompilerParams(
-            collective_id=0, has_side_effects=True, vmem_limit_bytes=57 * 1024 * 1024
+            collective_id=0, has_side_effects=True, vmem_limit_bytes=40 * 1024 * 1024
         ),
         cost_estimate=pl.CostEstimate(flops=10**9, bytes_accessed=12 * 10**6, transcendentals=0),
-    )(inputs.reshape(2, 4, 2, 128, 1792), out_grads, proj_in.T, proj_out.T, example_ids)
+    )(
+        *(
+            pltpu.with_memory_space_constraint(operand, pltpu.HBM)
+            for operand in (inputs.reshape(2, 4, 2, 128, 1792), out_grads, proj_in.T, proj_out.T, example_ids)
+        )
+    )
 
 
 def solution(mesh):

time: 30.5 us -> 28.8 us (0.944)
  local copies, waits for them, and re-layouts: 1.67 us -> 0.71 us
  Pallas kernels: 28.7 us -> 28 us
    unnamed x1, local copies, waits for them, and re-layouts: 1.67 us -> 0.71 us
    pallas_call x1, Pallas kernels: 28.7 us -> 28 us  [per_device(): pl.pallas_call(kernel, out_shape=pltpu.VMEM((256, 256), F32), in_specs=[h...]
where the time goes in v3:
time: 28.8 us; the launch traced here: 28.7 us
  Pallas kernels  28 us (97%)
  local copies, waits for them, and re-layouts  0.71 us (2%)
    pallas_call x1, Pallas kernels, per_device(): pl.pallas_call(kernel, out_shape=pltpu.VMEM((256, 256), F32), in_specs=[h...  28 us
    unnamed x1, local copies, waits for them, and re-layouts  0.71 us

profile of v3, /device:TPU:33, one launch (start us, length us, event | category | flops | bytes accessed | tf_op | source)
XLA Modules:
  0.0 28.7 jit_solution(16263714847186661235)
XLA Ops:
  0.0 28.0 %shard_map.55 = f32[256,256]{1,0:T(8,128)S(1)} custom-call(bf16[2,4,2,128,1792]{4,3,2,1,0:T(8,128)(2,1)} %bitcast.3, bf16[128,8192]{1,0:T(8,128)(2,1)} %og_hbm.1, bf16[64,1792]{1,0:T(8,128)(2,1)} %bitcast.5, bf16[64,8192]{1,0:T(8,128)(2,1)} %bitcast.4, s32[1,2048]{1,0:T(1,128)} %ids_hbm.1), custom_call_target="tpu_custom_call" | custom-call | flops 1000000000 | bytes 12000000 | tf_op jit(solution)/shard_map/pallas_call | solution.py:239
  28.0 0.7 %copy.7 = f32[256,256]{1,0:T(8,128)} copy(f32[256,256]{1,0:T(8,128)S(1)} %shard_map.55) | data formatting | bytes 524288

commit v4 on v3

--- a/solution.py
+++ b/solution.py
@@ -13,7 +13,7 @@
 NT = (((1,), (1,)), ((), ()))
 
 CHIPS = (6, 5, 7, 2, 4, 1, 3)
-TENSORS = (12, 13, 10, 11, 14, 15, 4, 5, 8, 9, 2, 3, 6, 7, 1)
+TENSORS = tuple(range(15, 0, -1))
 GROUPS = (10, 6, 14, 2, 9, 11, 5, 7, 13, 15, 1, 3, 8, 4, 12)
 
 
@@ -24,7 +24,7 @@
 
 def kernel(
     x_hbm, og_hbm, wi_hbm, wo_hbm, ids_hbm, out_ref,
-    x_v, og_v, wi_v, wo_v, ids_v, g_v, give, take, masked, pieces, shares, mine, cols, rows,
+    x_v, og_v, wi_v, wo_v, ids_v, g_v, give, take, halves, pieces, shares, mine, cols, rows,
     local_sem, x_sem, g_send, g_recv, s_send, s_recv, b_send, b_recv, c_send, last_send, col_recv, row_recv,
     x_known, z_known, all_known,
 ):
@@ -109,15 +109,10 @@
         s_copies[part - 2].wait_recv()
         total = sketch + take[part - 2]
         side = lax.bitwise_xor(z, part % 2)
-        ids = jnp.concatenate(
-            [ids_v[:, pl.ds(pl.multiple_of((8 * side + 2 * b + core) * 128, 128), 128)] for b in range(4)], axis=1
-        )
         high, low = split(total)
         lanes = slice(512 * (part - 2), 512 * (part - 1))
-        for e in range(EX_DEV):
-            own = ids == e
-            masked[64 * e : 64 * (e + 1), lanes] = jnp.where(own, high, jnp.zeros_like(high))
-            masked[256 + 64 * e : 256 + 64 * (e + 1), lanes] = jnp.where(own, low, jnp.zeros_like(low))
+        halves[:64, lanes] = high
+        halves[64:, lanes] = low
 
     pl.semaphore_wait(x_known, len(x_peers))
     for peer in z_peers:
@@ -128,18 +123,24 @@
         count = 3 if side == 0 else 4
         arrived = g_v.at[pl.ds(0, count)]
         pltpu.make_async_copy(arrived, arrived, g_recv.at[side]).wait()
-        grads = []
-        for b in range(4):
-            high, low = split(g_v[4 * side + b])
-            grads.append(jnp.concatenate([high, low], axis=0))
+        high, low = split(jnp.concatenate([g_v[4 * side + b] for b in range(4)], axis=1))
+        here = 8 * lax.bitwise_xor(z, side) + core
+        ids = jnp.concatenate(
+            [ids_v[:, pl.ds(pl.multiple_of((here + 2 * b) * 128, 128), 128)] for b in range(4)], axis=1
+        )
+        zero = jnp.zeros_like(high)
+        grads = jnp.concatenate(
+            [jnp.where(ids == e, part, zero) for e in range(EX_DEV) for part in (high, low)], axis=0
+        )
         term = lax.dot_general(
-            masked[:, 512 * side : 512 * (side + 1)], jnp.concatenate(grads, axis=1), NT, preferred_element_type=F32
+            halves[:, 512 * side : 512 * (side + 1)], grads, NT, preferred_element_type=F32
         )
         product = term if side == 0 else product + term
+    product = product[:64] + product[64:]
     lane = lax.broadcasted_iota(jnp.int32, (64, 128), 1)
     both = []
     for e in range(EX_DEV):
-        term = product[64 * e : 64 * (e + 1)] + product[256 + 64 * e : 256 + 64 * (e + 1)]
+        term = product[:, 128 * e : 128 * (e + 1)]
         both.append(term + pltpu.roll(term, 64, 1))
     first = jnp.where(lane < 64, both[0], both[1]).reshape(8, 8, 128)
     second = jnp.where(lane < 64, both[2], both[3]).reshape(8, 8, 128)
@@ -215,7 +216,9 @@
     lh, ll = split(left)
     rh, rl = split(right)
     dot = lambda a, b: jnp.dot(a, b, preferred_element_type=F32)
-    out_ref[...] = (dot(lh, rl) + dot(ll, rh) + dot(lh, rh)) * (1.0 / (64 * SEQ))
+    out_ref[...] = dot(
+        jnp.concatenate([lh, ll, lh], axis=1), jnp.concatenate([rl, rh, rh], axis=0)
+    ) * (1.0 / (64 * SEQ))
 
     for copy in s_copies:
         copy.wait_send()
@@ -250,7 +253,7 @@
             pltpu.VMEM((8, 64, 128), F32),
             pltpu.VMEM((2, 64, 512), F32),
             pltpu.VMEM((2, 64, 512), F32),
-            pltpu.VMEM((512, 1024), BF16),
+            pltpu.VMEM((128, 1024), BF16),
             pltpu.VMEM((16, 8, 128), F32),
             pltpu.VMEM((16, 8, 128), F32),
             pltpu.VMEM((8, 128), F32),

time: 28.8 us -> 28.6 us (level); the launches traced: 28.7 us -> 28.1 us
  Pallas kernels: 28 us -> 27.4 us
    pallas_call x1, Pallas kernels: 28 us -> 27.4 us  [per_device(): pl.pallas_call(kernel, out_shape=pltpu.VMEM((256, 256), F32), in_specs=[h...]
where the time goes in v4:
time: 28.6 us; the launch traced here: 28.1 us
  Pallas kernels  27.4 us (96%)
  local copies, waits for them, and re-layouts  0.71 us (2%)
    pallas_call x1, Pallas kernels, per_device(): pl.pallas_call(kernel, out_shape=pltpu.VMEM((256, 256), F32), in_specs=[h...  27.4 us
    unnamed x1, local copies, waits for them, and re-layouts  0.71 us

profile of v4, /device:TPU:33, one launch (start us, length us, event | category | flops | bytes accessed | tf_op | source)
XLA Modules:
  0.0 28.1 jit_solution(11073253901011774023)
XLA Ops:
  0.0 27.4 %shard_map.55 = f32[256,256]{1,0:T(8,128)S(1)} custom-call(bf16[2,4,2,128,1792]{4,3,2,1,0:T(8,128)(2,1)} %bitcast.3, bf16[128,8192]{1,0:T(8,128)(2,1)} %og_hbm.1, bf16[64,1792]{1,0:T(8,128)(2,1)} %bitcast.5, bf16[64,8192]{1,0:T(8,128)(2,1)} %bitcast.4, s32[1,2048]{1,0:T(1,128)} %ids_hbm.1), custom_call_target="tpu_custom_call" | custom-call | flops 1000000000 | bytes 12000000 | tf_op jit(solution)/shard_map/pallas_call | solution.py:242
  27.4 0.7 %copy.7 = f32[256,256]{1,0:T(8,128)} copy(f32[256,256]{1,0:T(8,128)S(1)} %shard_map.55) | data formatting | bytes 524288

commit v5 on v4

--- a/solution.py
+++ b/solution.py
@@ -24,7 +24,7 @@
 
 def kernel(
     x_hbm, og_hbm, wi_hbm, wo_hbm, ids_hbm, out_ref,
-    x_v, og_v, wi_v, wo_v, ids_v, g_v, give, take, halves, pieces, shares, mine, cols, rows,
+    x_v, og_v, wi_v, wo_v, ids_v, g_v, give, take, halves, pieces, shares, mine, cols, rows, final,
     local_sem, x_sem, g_send, g_recv, s_send, s_recv, b_send, b_recv, c_send, last_send, col_recv, row_recv,
     x_known, z_known, all_known,
 ):
@@ -202,22 +202,21 @@
     cols[dp] = piece
     others = cols.at[pl.ds(0, 15)]
     pltpu.make_async_copy(others, others, col_recv).wait()
+    c2 = cols[...].reshape(128, 128)
+    c_bit = (lax.broadcasted_iota(jnp.int32, (128, 128), 0) // 2) % 2
+    right = jnp.concatenate(
+        [jnp.where(c_bit == 0, c2, pltpu.roll(c2, 2, 0)), jnp.where(c_bit == 1, c2, pltpu.roll(c2, 126, 0))], axis=1
+    )
+    rh, rl = split(right)
+    final[...] = jnp.concatenate([rl, rh, rh], axis=0)
     pltpu.make_async_copy(rows, rows, row_recv).wait()
-
     r2 = rows[...].reshape(128, 128).T
-    c2 = cols[...].reshape(128, 128)
     r_bit = (lax.broadcasted_iota(jnp.int32, (128, 128), 1) // 2) % 2
-    c_bit = (lax.broadcasted_iota(jnp.int32, (128, 128), 0) // 2) % 2
     zero = jnp.zeros_like(r2)
     left = jnp.concatenate([jnp.where(r_bit == 0, r2, zero), jnp.where(r_bit == 1, r2, zero)], axis=0)
-    right = jnp.concatenate(
-        [jnp.where(c_bit == 0, c2, pltpu.roll(c2, 2, 0)), jnp.where(c_bit == 1, c2, pltpu.roll(c2, 126, 0))], axis=1
-    )
     lh, ll = split(left)
-    rh, rl = split(right)
-    dot = lambda a, b: jnp.dot(a, b, preferred_element_type=F32)
-    out_ref[...] = dot(
-        jnp.concatenate([lh, ll, lh], axis=1), jnp.concatenate([rl, rh, rh], axis=0)
+    out_ref[...] = jnp.dot(
+        jnp.concatenate([lh, ll, lh], axis=1), final[...], preferred_element_type=F32
     ) * (1.0 / (64 * SEQ))
 
     for copy in s_copies:
@@ -259,6 +258,7 @@
             pltpu.VMEM((8, 128), F32),
             pltpu.VMEM((16, 8, 128), F32),
             pltpu.VMEM((16, 8, 128), F32),
+            pltpu.VMEM((384, 256), BF16),
             dma((6,)), dma((4,)), dma, dma((2,)), dma((2,)), dma((2,)),
             dma, dma, dma, dma, dma, dma,
             regular, regular, regular,

time: 28.6 us -> 28.6 us (level)
  no operation moved by 1% of the time
where the time goes in v5:
time: 28.6 us; the launch traced here: 28.1 us
  Pallas kernels  27.4 us (96%)
  local copies, waits for them, and re-layouts  0.71 us (2%)
    pallas_call x1, Pallas kernels, per_device(): pl.pallas_call(kernel, out_shape=pltpu.VMEM((256, 256), F32), in_specs=[h...  27.4 us
    unnamed x1, local copies, waits for them, and re-layouts  0.71 us

profile of v5, /device:TPU:33, one launch (start us, length us, event | category | flops | bytes accessed | tf_op | source)
XLA Modules:
  0.0 28.1 jit_solution(8646436179800211059)
XLA Ops:
  0.0 27.4 %shard_map.55 = f32[256,256]{1,0:T(8,128)S(1)} custom-call(bf16[2,4,2,128,1792]{4,3,2,1,0:T(8,128)(2,1)} %bitcast.3, bf16[128,8192]{1,0:T(8,128)(2,1)} %og_hbm.1, bf16[64,1792]{1,0:T(8,128)(2,1)} %bitcast.5, bf16[64,8192]{1,0:T(8,128)(2,1)} %bitcast.4, s32[1,2048]{1,0:T(1,128)} %ids_hbm.1), custom_call_target="tpu_custom_call" | custom-call | flops 1000000000 | bytes 12000000 | tf_op jit(solution)/shard_map/pallas_call | solution.py:241
  27.4 0.7 %copy.7 = f32[256,256]{1,0:T(8,128)} copy(f32[256,256]{1,0:T(8,128)S(1)} %shard_map.55) | data formatting | bytes 524288

commit v6 on v5

--- a/solution.py
+++ b/solution.py
@@ -180,25 +180,25 @@
             src_ref=mine, dst_ref=rows.at[dp], send_sem=c_send, recv_sem=row_recv,
             device_id=(tensor, lax.bitwise_xor(tensor, r)), device_id_type=MESH,
         ).start()
+    last = pltpu.make_async_remote_copy(
+        src_ref=mine, dst_ref=rows.at[dp], send_sem=last_send, recv_sem=row_recv,
+        device_id=(tensor, tensor), device_id_type=MESH,
+    )
+    here = pltpu.make_async_copy(mine, rows.at[dp], row_recv)
+
+    @pl.when(tensor != dp)
+    def _():
+        last.start()
+
+    @pl.when(tensor == dp)
+    def _():
+        here.start()
+
     for r in GROUPS:
         pltpu.make_async_remote_copy(
             src_ref=mine, dst_ref=cols.at[dp], send_sem=c_send, recv_sem=col_recv,
             device_id=(lax.bitwise_xor(dp, r), tensor), device_id_type=MESH,
         ).start()
-    last = pltpu.make_async_remote_copy(
-        src_ref=mine, dst_ref=rows.at[dp], send_sem=last_send, recv_sem=row_recv,
-        device_id=(tensor, tensor), device_id_type=MESH,
-    )
-    here = pltpu.make_async_copy(mine, rows.at[dp], row_recv)
-
-    @pl.when(tensor != dp)
-    def _():
-        last.start()
-
-    @pl.when(tensor == dp)
-    def _():
-        here.start()
-
     cols[dp] = piece
     others = cols.at[pl.ds(0, 15)]
     pltpu.make_async_copy(others, others, col_recv).wait()

time: 28.6 us -> 28.6 us (level)
  no operation moved by 1% of the time
where the time goes in v6:
time: 28.6 us; the launch traced here: 28.1 us
  Pallas kernels  27.4 us (96%)
  local copies, waits for them, and re-layouts  0.71 us (2%)
    pallas_call x1, Pallas kernels, per_device(): pl.pallas_call(kernel, out_shape=pltpu.VMEM((256, 256), F32), in_specs=[h...  27.4 us
    unnamed x1, local copies, waits for them, and re-layouts  0.71 us

profile of v6, /device:TPU:33, one launch (start us, length us, event | category | flops | bytes accessed | tf_op | source)
XLA Modules:
  0.0 28.1 jit_solution(12536493355901343213)
XLA Ops:
  0.0 27.4 %shard_map.55 = f32[256,256]{1,0:T(8,128)S(1)} custom-call(bf16[2,4,2,128,1792]{4,3,2,1,0:T(8,128)(2,1)} %bitcast.3, bf16[128,8192]{1,0:T(8,128)(2,1)} %og_hbm.1, bf16[64,1792]{1,0:T(8,128)(2,1)} %bitcast.5, bf16[64,8192]{1,0:T(8,128)(2,1)} %bitcast.4, s32[1,2048]{1,0:T(1,128)} %ids_hbm.1), custom_call_target="tpu_custom_call" | custom-call | flops 1000000000 | bytes 12000000 | tf_op jit(solution)/shard_map/pallas_call | solution.py:241
  27.4 0.7 %copy.7 = f32[256,256]{1,0:T(8,128)} copy(f32[256,256]{1,0:T(8,128)S(1)} %shard_map.55) | data formatting | bytes 524288
